TPU v7x, 512 devices: a whole 4x8x8 slice. The times are simulated.
512 devices in a mesh: tile: 32 (over y, x), plane: 16 (over z, core).
Axes of the slice: x: 4, y: 8, z: 8, core: 2. Of those that a mesh axis runs over, the one named last changes fastest.
Arguments:
- slab_data: bfloat16 [512, 128, 2048], P('tile', 'plane'), may hold values from -24 to 24
- footprints: float32 [32768, 256], P(('tile', 'plane')), may hold values from 0 to 4
- traces: float32 [32768, 128], P(('tile', 'plane')), may hold values from -6 to 6
- corners: int32 [32768, 2], P(('tile', 'plane')), may hold values from 0 to 112, as said below
- counts: int32 [512], P(('tile', 'plane')), may hold values from 32 to 64, as said below
Outputs:
- updated_footprints: float32 [32768, 256], P(('tile', 'plane'))
Inputs may be any that keep to these rules, and one draw needn't show every extreme that they name: corners[n, 0] lies in 0 to 112 and corners[n, 1] in 0 to 15, so a box may run into the next tile; both ends are taken in every draw. `counts`: some owner has 64 live neurons and some has 32 in every draw.
All inputs are finite; a program needn't handle non-finite values.
Results may differ from a plain program's by a relative error of at most 0.0028.
Values may be sent and summed in bfloat16 or wider, within the bound.
A program may use at most 192 MiB of HBM per device.

v0:
```python
import jax
import jax.numpy as jnp
from jax import lax
from jax.sharding import PartitionSpec as P

PR = 16
PC = 16
SWEEPS = 2
GROUPS = 2


def from_behind(x, axis, by):
    size = lax.axis_size(axis)
    pairs = [(i, i + by) for i in range(size) if 0 <= i + by < size]
    return lax.ppermute(x, axis, pairs)


def update_region(
    signal, row_count, column_count, patches, trace_rows, top_rows, left_columns, alive_flags
):
    slot_count, patch_rows, patch_columns = patches.shape
    row_hit = (
        jnp.arange(row_count)[None, :, None]
        == top_rows[:, None, None] + jnp.arange(patch_rows)[None, None, :]
    ).astype(jnp.float32) * alive_flags[:, None, None]
    column_hit = (
        jnp.arange(column_count)[None, :, None]
        == left_columns[:, None, None] + jnp.arange(patch_columns)[None, None, :]
    ).astype(jnp.float32)
    spread = jnp.einsum("sij,scj->sic", patches, column_hit, precision=lax.Precision.HIGHEST)
    current = jnp.einsum("sri,sic->rcs", row_hit, spread, precision=lax.Precision.HIGHEST).reshape(
        row_count * column_count, slot_count
    )
    support = (
        jnp.sum(row_hit, axis=2).T[:, None, :] * jnp.sum(column_hit, axis=2).T[None, :, :]
    ).reshape(row_count * column_count, slot_count)
    gram = jnp.dot(trace_rows, trace_rows.T, precision=lax.Precision.HIGHEST)
    scaling = jnp.where(alive_flags > 0.5, jnp.diagonal(gram), jnp.ones_like(alive_flags))
    group_width = slot_count // (2 * GROUPS)
    split_shape = (row_count * column_count, 2, GROUPS, group_width)
    signal_blocks = signal.reshape(split_shape)
    support_blocks = support.reshape(split_shape)
    scale_blocks = scaling.reshape(2, GROUPS, group_width)
    gram_blocks = gram.reshape(slot_count, 2, GROUPS, group_width)
    for repeat_index in range(SWEEPS):
        for group_index in range(GROUPS):
            columns_used = gram_blocks[:, :, group_index, :].reshape(slot_count, 2 * group_width)
            mixed = jnp.dot(current, columns_used, precision=lax.Precision.HIGHEST).reshape(
                row_count * column_count, 2, group_width
            )
            blocked = current.reshape(split_shape)
            fresh = support_blocks[:, :, group_index, :] * jnp.maximum(
                blocked[:, :, group_index, :]
                + (signal_blocks[:, :, group_index, :] - mixed) / scale_blocks[:, group_index, :],
                0.0,
            )
            current = (
                blocked.at[:, :, group_index, :]
                .set(fresh)
                .reshape(row_count * column_count, slot_count)
            )
    current = current.reshape(row_count, column_count, slot_count)
    picked = jnp.einsum("sri,rcs->sic", row_hit, current, precision=lax.Precision.HIGHEST)
    return jnp.einsum("sic,scj->sij", picked, column_hit, precision=lax.Precision.HIGHEST)


def body(slab_data, footprints, traces, corners, counts):
    column_count = slab_data.shape[0]
    row_count = slab_data.shape[2] // lax.axis_size("plane")
    slot_count = footprints.shape[0]
    local_index = jnp.arange(slot_count)
    corner_float = corners.astype(jnp.float32)
    count_float = counts.astype(jnp.float32)
    own_patch = footprints.reshape(slot_count, PR, PC)
    own_alive = (local_index < count_float[0]).astype(jnp.float32)
    left_patch, left_trace, left_corner, left_count = from_behind(
        (footprints, traces, corner_float, count_float), "tile", 1
    )
    left_alive = (local_index < left_count[0]).astype(jnp.float32)
    slot_trace = jnp.concatenate([left_trace, traces], axis=0)
    slot_top_float = jnp.concatenate([left_corner[:, 0], corner_float[:, 0]], axis=0)
    slot_top = slot_top_float.astype(jnp.int32)
    data_block = lax.all_to_all(slab_data, "plane", split_axis=2, concat_axis=1, tiled=True)
    signal = jnp.einsum(
        "cfr,sf->rcs",
        data_block,
        slot_trace.astype(jnp.bfloat16),
        preferred_element_type=jnp.float32,
    ).reshape(row_count * column_count, 2 * slot_count)
    pieces = update_region(
        signal,
        row_count,
        column_count,
        jnp.concatenate([left_patch.reshape(slot_count, PR, PC), own_patch], axis=0),
        slot_trace,
        slot_top,
        jnp.concatenate(
            [left_corner[:, 1].astype(jnp.int32) - column_count, corners[:, 1]], axis=0
        ),
        jnp.concatenate([left_alive, own_alive], axis=0),
    )
    own_piece = pieces[slot_count:].reshape(slot_count, PR * PC)
    returned = from_behind(pieces[:slot_count].reshape(slot_count, PR * PC), "tile", -1)
    return own_piece + returned


def solution(mesh):
    in_specs = (
        P("tile", "plane", None),
        P(("tile", "plane"), None),
        P(("tile", "plane"), None),
        P(("tile", "plane"), None),
        P(("tile", "plane")),
    )
    out_specs = P(("tile", "plane"), None)
    return jax.shard_map(body, mesh=mesh, in_specs=in_specs, out_specs=out_specs, check_vma=False)
```

profile of v0, /device:TPU:30, one launch (start us, length us, event | category | flops | bytes accessed | tf_op | source)
XLA Modules:
  0.0 153.1 jit_solution(12663454522602324248)
XLA Ops:
  0.7 5.9 %collective-permute-start.1 = (f32[1]{0:T(128)}, f32[1]{0:T(128)}, u32[]{:S(2)}, u32[]{:S(2)}) collective-permute-start(f32[1]{0:T(128)} %convert_element_type.57), channel_id=1, source_target_pairs={{0,16},{16,32},{32,48},{48,64},{64,80},{80,96},{96,112},{112,128},... | collective-permute-start | bytes 20 | tf_op jit(solution)/shard_map/ppermute | solution.py:15
  6.5 0.7 convert_element_type.54
  7.2 3.4 %collective-permute-start = (f32[64,2]{0,1:T(2,128)S(1)}, f32[64,2]{0,1:T(2,128)S(1)}, u32[]{:S(2)}, u32[]{:S(2)}) collective-permute-start(f32[64,2]{0,1:T(2,128)S(1)} %convert_element_type.54), channel_id=1, source_target_pairs={{0,16},{16,32},{32,48},{48,64},{64,80},{80,96},{96,112},{112,128},... | collective-permute-start | bytes 1544 | tf_op jit(solution)/shard_map/ppermute | solution.py:15
  10.6 3.4 %collective-permute-start.3 = (f32[64,128]{1,0:T(8,128)}, f32[64,128]{1,0:T(8,128)S(1)}, u32[]{:S(2)}, u32[]{:S(2)}) collective-permute-start(f32[64,128]{1,0:T(8,128)} %param.15), channel_id=1, source_target_pairs={{0,16},{16,32},{32,48},{48,64},{64,80},{80,96},{96,112},{112,128},... | collective-permute-start | bytes 98312 | tf_op jit(solution)/shard_map/ppermute | solution.py:15
  14.0 0.9 copy.57
  15.0 3.1 %collective-permute-start.2 = (f32[64,256]{0,1:T(8,128)S(1)}, f32[64,256]{0,1:T(8,128)S(1)}, u32[]{:S(2)}, u32[]{:S(2)}) collective-permute-start(f32[64,256]{0,1:T(8,128)S(1)} %copy.57), channel_id=1, source_target_pairs={{0,16},{16,32},{32,48},{48,64},{64,80},{80,96},{96,112},{112,128},... | collective-permute-start | bytes 196616 | tf_op jit(solution)/shard_map/ppermute | solution.py:15
  18.1 5.5 %copy.66 = bf16[16,8,2048]{0,1,2:T(8,128)(2,1)} copy(bf16[16,8,2048]{2,1,0:T(8,128)(2,1)} %param.13) | data formatting | bytes 1048576 | tf_op args[0]
  23.6 6.4 %reshape.294 = bf16[16,2,8192]{2,1,0:T(2,128)(2,1)} reshape(bf16[2048,8,16]{2,1,0:T(8,128)(2,1)} %bitcast.112) | data formatting | bytes 1048576
  30.0 10.5 %all-to-all-start = ((bf16[16,2,8192]{2,1,0:T(2,128)(2,1)}), bf16[16,2,8192]{2,1,0:T(2,128)(2,1)}, u32[]{:S(2)}, u32[]{:S(2)}) async-start(bf16[16,2,8192]{2,1,0:T(2,128)(2,1)} %reshape.294), calls=%async_computation | async-start | bytes 1048576 | tf_op jit(solution)/shard_map/all_to_all | solution.py:83
  40.6 0.7 convert_compare_fusion.1
  41.3 0.7 convert_compare_fusion.3
  42.0 0.1 add_convert_fusion.1
  42.1 0.1 pad_add_fusion
  42.2 0.1 iota_add_fusion
  42.3 0.1 maximum_convert_fusion
  42.3 0.1 iota_add_fusion.1
  42.4 0.9 select_reduce_fusion
  43.4 0.1 copy.62
  43.5 0.4 convert_reduce_fusion
  43.8 0.1 copy.63
  43.9 0.1 broadcast_multiply_fusion
  44.0 4.6 %mul.42 = f32[2048,2,2,32]{3,2,1,0:T(2,128)} reshape(f32[128,16,128]{2,1,0:T(8,128)S(1)} %broadcast_multiply_fusion) | data formatting | bytes 2097152 | tf_op jit(solution)/shard_map/mul | solution.py:35
  48.6 7.6 %fusion.46 = (f32[2048,2,1,32]{3,2,1,0:T(1,128)}, f32[2048,2,1,32]{3,2,1,0:T(1,128)S(1)}) fusion(f32[2048,2,2,32]{3,2,1,0:T(2,128)} %mul.42), kind=kLoop, calls=%fused_computation.82 | loop fusion | bytes 2097152 | tf_op jit(solution)/shard_map/slice | solution.py:52
  56.2 5.6 %copy.94 = f32[2048,2,1,32]{0,3,1,2:T(8,128)} copy(f32[2048,2,1,32]{3,2,1,0:T(1,128)} %get-tuple-element.53) | data formatting | bytes 1048576
  61.8 2.3 %copy.92 = f32[2048,2,1,32]{0,3,1,2:T(8,128)S(1)} copy(f32[2048,2,1,32]{3,2,1,0:T(1,128)S(1)} %get-tuple-element.54) | data formatting | bytes 1048576
  64.2 0.3 fusion.50
  64.4 1.3 gather_fusion
  65.7 0.1 gather.7
  65.8 0.1 pad_maximum_fusion
  66.0 0.5 copy.59
  66.4 1.1 fusion.32
  67.5 1.5 fusion.28
  69.1 0.7 copy.61
  69.8 4.6 %reshape_reshape.10 = f32[2048,2,2,32]{3,2,1,0:T(2,128)} reshape(f32[128,16,128]{2,1,0:T(8,128)S(1)} %copy.61) | data formatting | bytes 2097152 | tf_op jit(solution)/shard_map/reshape;reshape | solution.py:51
  74.4 5.2 %copy.71 = f32[2048,2,2,32]{0,3,1,2:T(8,128)S(1)} copy(f32[2048,2,2,32]{3,2,1,0:T(2,128)} %reshape_reshape.10) | data formatting | bytes 2097152 | tf_op jit(solution)/shard_map/reshape;reshape | solution.py:51
  79.5 0.8 slice_bitcast_fusion.3
  80.4 5.4 %reshape.295 = bf16[2048,8,16]{2,1,0:T(8,128)(2,1)} reshape(bf16[16,2,8192]{2,1,0:T(2,128)(2,1)} %all-to-all-done) | data formatting | bytes 1048576
  85.8 5.3 %copy.67 = bf16[16,8,16,128]{3,1,2,0:T(8,128)(2,1)} copy(bf16[16,8,16,128]{0,1,3,2:T(8,128)(2,1)} %bitcast.111) | data formatting | bytes 1048576 | tf_op jit(solution)/shard_map/all_to_all | solution.py:83
  91.1 2.3 %convolution_bitcast_fusion = f32[128,16,128]{0,2,1:T(8,128)} fusion(bf16[16,8,16,128]{3,1,2,0:T(8,128)(2,1)} %copy.67, f32[128,128]{1,0:T(8,128)S(1)} %constant_dynamic-update-slice_fusion), kind=kOutput, calls=%fused_computation.34 | convolution fusion | flops 67125248 | bytes 1638400 | tf_op jit(solution)/shard_map/cfr,sf->rcs/dot_general | solution.py:84
  93.4 2.6 %copy.68 = f32[128,16,128]{2,1,0:T(8,128)} copy(f32[128,16,128]{0,2,1:T(8,128)} %convolution_bitcast_fusion) | data formatting | bytes 2097152 | tf_op jit(solution)/shard_map/cfr,sf->rcs/transpose | solution.py:84
  96.0 5.8 %reshape_reshape.11 = f32[2048,2,2,32]{3,2,1,0:T(2,128)} reshape(f32[128,16,128]{2,1,0:T(8,128)} %copy.68) | data formatting | bytes 2097152 | tf_op jit(solution)/shard_map/reshape;reshape | solution.py:41
  101.8 8.0 %fusion.47 = (f32[2048,2,1,32]{3,2,1,0:T(1,128)}, f32[2048,2,1,32]{3,2,1,0:T(1,128)}) fusion(f32[2048,2,2,32]{3,2,1,0:T(2,128)} %reshape_reshape.11), kind=kLoop, calls=%fused_computation.83 | loop fusion | bytes 2097152 | tf_op jit(solution)/shard_map/slice | solution.py:54
  109.8 5.6 %copy.93 = f32[2048,2,1,32]{0,3,1,2:T(8,128)} copy(f32[2048,2,1,32]{3,2,1,0:T(1,128)} %get-tuple-element.56) | data formatting | bytes 1048576
  115.4 2.5 %fusion.5 = f32[2048,2,2,32]{0,3,1,2:T(8,128)S(1)} fusion(f32[2048,2,2,32]{0,3,1,2:T(8,128)S(1)} %copy.71, f32[2048,2,32]{0,2,1:T(8,128)} %slice_bitcast_fusion.3, f32[2048,128,1]{1,0,2:T(8,128)S(1)} %bitcast.113, f32[2048,2,1,32]{0,3,1,2:T(8,128)} %copy.93, f32[2048,2,1,32]{0,3,1,2:T(8,128)S(1)} %copy.92, f32[2,32]{1,0:T(2,128)S(1)} %bitcast.128, ...), kind=kOutput, calls=%fused_computation.10 | convolution fusion | flops 201981952 | bytes 3179520 | tf_op jit(solution)/shard_map/dot_general | solution.py:48
  117.9 0.8 slice_bitcast_fusion.2
  118.8 1.0 copy.74
  119.8 4.0 %copy.95 = f32[2048,2,1,32]{0,3,1,2:T(8,128)} copy(f32[2048,2,1,32]{3,2,1,0:T(1,128)S(1)} %copy-done) | data formatting | bytes 1048576
  123.8 2.5 %fusion.11 = f32[2048,2,2,32]{0,3,1,2:T(8,128)S(1)} fusion(f32[2048,2,2,32]{0,3,1,2:T(8,128)S(1)} %fusion.5, f32[2048,2,32]{0,2,1:T(8,128)} %slice_bitcast_fusion.2, f32[2048,128,1]{0,1,2:T(8,128)} %bitcast.118, f32[2048,2,1,32]{0,3,1,2:T(8,128)} %copy.95, f32[2048,2,1,32]{0,3,1,2:T(8,128)} %copy.94, f32[2,32]{1,0:T(2,128)S(1)} %bitcast.126, ...), kind=kOutput, calls=%fused_computation.16 | convolution fusion | flops 201981952 | bytes 3179520 | tf_op jit(solution)/shard_map/dot_general | solution.py:48
  126.4 0.1 copy.76
  126.5 0.8 fusion.17
  127.3 0.1 copy.78
  127.4 0.2 copy-done.4
  127.6 0.8 fusion.23
  128.3 4.3 %copy.80 = f32[2048,2,2,32]{3,2,1,0:T(2,128)} copy(f32[2048,2,2,32]{0,3,1,2:T(8,128)S(1)} %fusion.23) | data formatting | bytes 2097152 | tf_op jit(solution)/shard_map/scatter | solution.py:59
  132.7 4.8 %reshape_reshape.12 = f32[128,16,128]{2,1,0:T(8,128)S(1)} reshape(f32[2048,2,2,32]{3,2,1,0:T(2,128)} %copy.80) | data formatting | bytes 2097152 | tf_op jit(solution)/shard_map/reshape;reshape | solution.py:62
  137.5 0.7 copy.81
  138.2 2.2 %fusion.24 = f32[128,16,16]{2,1,0:T(8,128)S(1)} fusion(f32[128,16,128]{0,1,2:T(8,128)S(1)} %copy.81, f32[128]{0:T(128)S(1)} %add_convert_fusion.1, s32[128,16]{1,0:T(8,128)S(1)} %iota_add_fusion.1), kind=kOutput, calls=%fused_computation.29 | convolution fusion | flops 50855936 | bytes 1188352 | tf_op jit(solution)/shard_map/sri,rcs->sic/dot_general | solution.py:63
  140.3 0.8 fusion.31
  141.1 0.1 fusion.48
  141.2 0.2 copy.83
  141.4 2.7 %collective-permute-start.4 = (f32[64,256]{0,1:T(8,128)S(1)}, f32[64,256]{0,1:T(8,128)S(1)}, u32[]{:S(2)}, u32[]{:S(2)}) collective-permute-start(f32[64,256]{0,1:T(8,128)S(1)} %bitcast.125), channel_id=1, source_target_pairs={{16,0},{32,16},{48,32},{64,48},{80,64},{96,80},{112,96},{128,112},... | collective-permute-start | bytes 196616 | tf_op jit(solution)/shard_map/ppermute | solution.py:15
  144.2 0.2 copy.82
  144.4 8.0 %collective-permute-done.4 = f32[64,256]{0,1:T(8,128)S(1)} collective-permute-done((f32[64,256]{0,1:T(8,128)S(1)}, f32[64,256]{0,1:T(8,128)S(1)}, u32[]{:S(2)}, u32[]{:S(2)}) %collective-permute-start.4) | collective-permute-done | bytes 65568 | tf_op jit(solution)/shard_map/ppermute | solution.py:15
  152.4 0.7 copy.84
  (34 shorter events, 0.2 us)
Async XLA Ops:
  0.7 39.9 %collective-permute-start.1 = (f32[1]{0:T(128)}, f32[1]{0:T(128)}, u32[]{:S(2)}, u32[]{:S(2)}) collective-permute-start(f32[1]{0:T(128)} %convert_element_type.57), channel_id=1, source_target_pairs={{0,16},{16,32},{32,48},{48,64},{64,80},{80,96},{96,112},{112,128},... | collective-permute-start | bytes 20 | tf_op jit(solution)/shard_map/ppermute | solution.py:15
  7.2 34.8 %collective-permute-start = (f32[64,2]{0,1:T(2,128)S(1)}, f32[64,2]{0,1:T(2,128)S(1)}, u32[]{:S(2)}, u32[]{:S(2)}) collective-permute-start(f32[64,2]{0,1:T(2,128)S(1)} %convert_element_type.54), channel_id=1, source_target_pairs={{0,16},{16,32},{32,48},{48,64},{64,80},{80,96},{96,112},{112,128},... | collective-permute-start | bytes 1544 | tf_op jit(solution)/shard_map/ppermute | solution.py:15
  10.6 53.5 %collective-permute-start.3 = (f32[64,128]{1,0:T(8,128)}, f32[64,128]{1,0:T(8,128)S(1)}, u32[]{:S(2)}, u32[]{:S(2)}) collective-permute-start(f32[64,128]{1,0:T(8,128)} %param.15), channel_id=1, source_target_pairs={{0,16},{16,32},{32,48},{48,64},{64,80},{80,96},{96,112},{112,128},... | collective-permute-start | bytes 98312 | tf_op jit(solution)/shard_map/ppermute | solution.py:15
  15.0 25.6 %copy-start.7 = (s32[64,2]{0,1:T(2,128)S(1)}, s32[64,2]{0,1:T(2,128)}, u32[]{:S(2)}) copy-start(s32[64,2]{0,1:T(2,128)} %param.16) | copy-start | bytes 1540
  15.0 50.9 %collective-permute-start.2 = (f32[64,256]{0,1:T(8,128)S(1)}, f32[64,256]{0,1:T(8,128)S(1)}, u32[]{:S(2)}, u32[]{:S(2)}) collective-permute-start(f32[64,256]{0,1:T(8,128)S(1)} %copy.57), channel_id=1, source_target_pairs={{0,16},{16,32},{32,48},{48,64},{64,80},{80,96},{96,112},{112,128},... | collective-permute-start | bytes 196616 | tf_op jit(solution)/shard_map/ppermute | solution.py:15
  30.0 50.4 %all-to-all-start = ((bf16[16,2,8192]{2,1,0:T(2,128)(2,1)}), bf16[16,2,8192]{2,1,0:T(2,128)(2,1)}, u32[]{:S(2)}, u32[]{:S(2)}) async-start(bf16[16,2,8192]{2,1,0:T(2,128)(2,1)} %reshape.294), calls=%async_computation | async-start | bytes 1048576 | tf_op jit(solution)/shard_map/all_to_all | solution.py:83
  56.2 8.0 %copy-start.6 = (f32[64,128]{1,0:T(8,128)S(1)}, f32[64,128]{1,0:T(8,128)}, u32[]{:S(2)}) copy-start(f32[64,128]{1,0:T(8,128)} %param.15) | copy-start | bytes 98308
  64.1 51.3 %copy-start.2 = (f32[2048,2,1,32]{0,3,1,2:T(8,128)}, f32[2048,2,1,32]{0,3,1,2:T(8,128)S(1)}, u32[]{:S(2)}) copy-start(f32[2048,2,1,32]{0,3,1,2:T(8,128)S(1)} %copy.92) | copy-start | bytes 1572868
  117.9 1.9 %copy-start = (f32[2048,2,1,32]{3,2,1,0:T(1,128)S(1)}, f32[2048,2,1,32]{3,2,1,0:T(1,128)}, u32[]{:S(2)}) copy-start(f32[2048,2,1,32]{3,2,1,0:T(1,128)} %get-tuple-element.55) | copy-start | bytes 1572868
  123.8 2.7 %copy-start.3 = (f32[2048,2,1,32]{0,3,1,2:T(8,128)S(1)}, f32[2048,2,1,32]{0,3,1,2:T(8,128)}, u32[]{:S(2)}) copy-start(f32[2048,2,1,32]{0,3,1,2:T(8,128)} %copy-done.2) | copy-start | bytes 1572868
  123.8 2.7 %copy-start.5 = (f32[2048,2,1,32]{0,3,1,2:T(8,128)S(1)}, f32[2048,2,1,32]{0,3,1,2:T(8,128)}, u32[]{:S(2)}) copy-start(f32[2048,2,1,32]{0,3,1,2:T(8,128)} %copy.93) | copy-start | bytes 1572868
  126.4 1.0 copy-start.1
  126.4 1.2 copy-start.4
  141.4 10.9 %collective-permute-start.4 = (f32[64,256]{0,1:T(8,128)S(1)}, f32[64,256]{0,1:T(8,128)S(1)}, u32[]{:S(2)}, u32[]{:S(2)}) collective-permute-start(f32[64,256]{0,1:T(8,128)S(1)} %bitcast.125), channel_id=1, source_target_pairs={{16,0},{32,16},{48,32},{64,48},{80,64},{96,80},{112,96},{128,112},... | collective-permute-start | bytes 196616 | tf_op jit(solution)/shard_map/ppermute | solution.py:15
where the time goes:
time: 154 us; the launch traced here: 153 us
  local copies, waits for them, and re-layouts  96.4 us (63%)
  starting transfers between devices  29 us (19%)
  matrix products  14.6 us (9%)
  waiting for transfers between devices  7.98 us (5%)
  other arithmetic  4 us (3%)
    unnamed x25, local copies, waits for them, and re-layouts  36 us
    ppermute x5, starting transfers between devices, from_behind(): return lax.ppermute(x, axis, pairs)  18.5 us
    all_to_all x1, starting transfers between devices, body(): lax.all_to_all(slab_data, 'plane', split_axis=2, concat_axis=1, tiled=True)  10.5 us
    another operation x2, local copies, waits for them, and re-layouts, update_region(): blocked = current.reshape(split_shape)  9.79 us
    slice x1, local copies, waits for them, and re-layouts, update_region(): signal_blocks[:, :, group_index, :] - mixed  8.03 us
    ppermute x5, waiting for transfers between devices, from_behind(): return lax.ppermute(x, axis, pairs)  7.98 us
    slice x1, local copies, waits for them, and re-layouts, update_region(): support_blocks[:, :, group_index, :]  7.56 us
    dot_general x4, matrix products, update_region(): jnp.dot(current, columns_used, precision=lax.Precision.HIGHEST)  6.54 us
  transfers between devices with their start and end apart: 6, of which 1 were waited for; matrix products, arithmetic and copies ran while one was open for 35% of the time, Pallas kernels for 0%

commit v1 on v0

v1 whole, which is shorter than its diff:
```python
import functools

import jax
import jax.numpy as jnp
from jax import lax
from jax.experimental import pallas as pl
from jax.experimental.pallas import tpu as pltpu
from jax.sharding import PartitionSpec as P

PR = 16
PC = 16
SWEEPS = 2
GROUPS = 2
CHUNK = 4
MESH = pl.DeviceIdType.MESH
GONE = 1 << 14


def mixed_order(left, own):
    half = own.shape[0] // GROUPS
    parts = []
    for g in range(GROUPS):
        parts += [left[g * half : (g + 1) * half], own[g * half : (g + 1) * half]]
    return jnp.concatenate(parts, axis=0)


def unmixed(x):
    quarter = x.shape[0] // (2 * GROUPS)
    blocks = [x[i * quarter : (i + 1) * quarter] for i in range(2 * GROUPS)]
    return jnp.concatenate(blocks[0::2], axis=0), jnp.concatenate(blocks[1::2], axis=0)


def column_of(row):
    n = row.shape[1]
    eye = lax.broadcasted_iota(jnp.int32, (n, n), 0) == lax.broadcasted_iota(jnp.int32, (n, n), 1)
    spread = jnp.where(eye, jnp.broadcast_to(row.astype(jnp.float32), (n, n)), 0.0)
    return jnp.sum(spread, axis=1, keepdims=True).astype(jnp.int32)


def split(x):
    high = x.astype(jnp.bfloat16)
    return high, (x - high.astype(jnp.float32)).astype(jnp.bfloat16)


def kernel(
    n_tile, n_plane, slab, fp, tr, corners, counts, own_out, ret_out,
    buf, own_fp, nb_fp, own_tr, nb_tr, own_corner, own_meta, nb_meta, own_count,
    patch, dense, base_s, step_s, weights, pieces, left_piece,
    load_sem, send_sem, recv_sem, side_send, side_recv, ret_send, ret_recv,
):
    cols, rows = buf.shape[1], buf.shape[3]
    slots = own_fp.shape[0]
    n_chunk = cols // CHUNK
    tile, me = lax.axis_index("tile"), lax.axis_index("plane")
    right = lax.rem(tile + 1, n_tile)
    left = lax.rem(tile + n_tile - 1, n_tile)

    barrier = pltpu.get_barrier_semaphore()

    @pl.loop(1, n_plane)
    def _(k):
        pl.semaphore_signal(
            barrier, inc=1, device_id={"plane": lax.rem(me + k, n_plane)}, device_id_type=MESH
        )

    for other in (left, right):
        pl.semaphore_signal(barrier, inc=1, device_id={"tile": other}, device_id_type=MESH)
    pl.semaphore_wait(barrier, n_plane + 1)

    def side(i, src, dst):
        return pltpu.make_async_remote_copy(
            src, dst, side_send.at[i], side_recv.at[i], device_id={"tile": right}, device_id_type=MESH
        )

    side_fp, side_tr = side(0, fp, nb_fp), side(1, tr, nb_tr)
    side_meta = side(2, own_meta, nb_meta)
    side_fp.start()
    side_tr.start()
    loads = [
        pltpu.make_async_copy(src, dst, load_sem.at[i])
        for i, (src, dst) in enumerate(
            ((corners, own_corner), (counts, own_count), (tr, own_tr), (fp, own_fp))
        )
    ]
    for load in loads:
        load.start()

    @pl.loop(0, n_chunk)
    def _(q):
        columns = pl.ds(q * CHUNK, CHUNK)

        @pl.loop(1, n_plane)
        def _(k):
            peer = lax.rem(me + k, n_plane)
            pltpu.make_async_remote_copy(
                slab.at[columns, :, pl.ds(pl.multiple_of(peer * rows, rows), rows)],
                buf.at[me, columns],
                send_sem.at[q],
                recv_sem.at[q],
                device_id={"plane": peer},
                device_id_type=MESH,
            ).start()

        pltpu.make_async_copy(
            slab.at[columns, :, pl.ds(pl.multiple_of(me * rows, rows), rows)],
            buf.at[me, columns],
            recv_sem.at[q],
        ).start()

    loads[0].wait()
    loads[1].wait()
    lane = lax.broadcasted_iota(jnp.int32, (1, slots), 1)
    own_meta[...] = jnp.zeros_like(own_meta)
    own_meta[0:1, 0:slots] = own_corner[0:1, :]
    own_meta[1:2, 0:slots] = jnp.where(lane < own_count[0, 0], own_corner[1:2, :], GONE)
    side_meta.start()
    loads[2].wait()
    loads[3].wait()
    side_meta.wait_recv()
    side_tr.wait_recv()
    side_fp.wait_recv()

    gone = jnp.where(tile > 0, -cols, GONE)
    top = mixed_order(column_of(nb_meta[0:1, 0:slots]), column_of(own_meta[0:1, 0:slots]))
    first = mixed_order(
        column_of(nb_meta[1:2, 0:slots]) + gone, column_of(own_meta[1:2, 0:slots])
    )
    alive = first < cols
    patch[...] = mixed_order(nb_fp[...], own_fp[...])
    trace = mixed_order(nb_tr[...], own_tr[...])
    both = 2 * slots
    gram = lax.dot_general(
        trace, trace, (((1,), (1,)), ((), ())),
        precision=lax.Precision.HIGHEST, preferred_element_type=jnp.float32,
    )
    eye = lax.broadcasted_iota(jnp.int32, (both, both), 0) == lax.broadcasted_iota(
        jnp.int32, (both, both), 1
    )
    diagonal = jnp.sum(jnp.where(eye, gram, 0.0), axis=1, keepdims=True)
    scale = jnp.where(alive, diagonal, 1.0)
    high, low = split(jnp.where(eye, 0.0, gram) / scale)
    for g in range(GROUPS):
        at = slice(g * slots, (g + 1) * slots)
        weights[g, 0:slots, 0:both] = high[at]
        weights[g, 0:slots, both : 2 * both] = high[at]
        weights[g, slots:both, 0:both] = low[at]
        weights[g, slots:both, both : 2 * both] = jnp.zeros((slots, both), jnp.bfloat16)
    trace_bf = trace.astype(jnp.bfloat16)
    inverse = jnp.broadcast_to(1.0 / scale, (both, rows))

    row = lax.broadcasted_iota(jnp.int32, (both, rows), 1)
    i_at = row - top
    in_rows = (i_at >= 0) & (i_at < PR)
    base_s[...] = jnp.where(in_rows, i_at, -1)
    step_s[...] = jnp.broadcast_to(first, (both, rows))

    def box_of(c):
        i_of = base_s[...]
        j_of = c - step_s[...]
        inside = (i_of >= 0) & (j_of >= 0) & (j_of < PC)
        return i_of, j_of, inside

    @pl.loop(0, cols)
    def _(c):
        i_of, j_of, inside = box_of(c)
        at = (i_of & 7) * PC + (j_of & (PC - 1))
        lower = jnp.take_along_axis(patch[:, 0:128], at, axis=1)
        upper = jnp.take_along_axis(patch[:, 128:256], at, axis=1)
        dense[c] = jnp.where(inside, jnp.where(i_of >= 8, upper, lower), 0.0)

    pieces[...] = jnp.zeros_like(pieces)
    lane_row = lax.broadcasted_iota(jnp.int32, (both, 128), 1)
    j_lane = lane_row & (PC - 1)
    pick_low = jnp.broadcast_to(top, (both, 128)) + (lane_row >> 4)

    @pl.loop(0, n_chunk)
    def _(q):
        c0 = q * CHUNK
        landed = buf.at[:, pl.ds(c0, CHUNK)]
        pltpu.make_async_copy(landed, landed, recv_sem.at[q]).wait()
        data, signal, now = [], [], []
        for c in range(CHUNK):
            block = buf[:, c0 + c].astype(jnp.float32)
            data.append(block.reshape(-1, rows).astype(jnp.bfloat16))
        summed = jnp.dot(
            trace_bf, jnp.concatenate(data, axis=1), preferred_element_type=jnp.float32
        )
        for c in range(CHUNK):
            _, _, inside = box_of(c0 + c)
            signal.append(
                jnp.where(inside, summed[:, c * rows : (c + 1) * rows] * inverse, -jnp.inf)
            )
            now.append(dense[c0 + c])
        signal = jnp.concatenate(signal, axis=1)
        now = jnp.concatenate(now, axis=1)
        now = [now[g * slots : (g + 1) * slots] for g in range(GROUPS)]
        parts = [split(x) for x in now]
        for _ in range(SWEEPS):
            for g in range(GROUPS):
                stacked = jnp.concatenate([p[0] for p in parts] + [p[1] for p in parts], axis=0)
                product = jnp.dot(weights[g], stacked, preferred_element_type=jnp.float32)
                mixed = product[0:slots] + product[slots:both]
                now[g] = jnp.maximum(signal[g * slots : (g + 1) * slots] - mixed, 0.0)
                parts[g] = split(now[g])
        done = jnp.concatenate(now, axis=0)
        for c in range(CHUNK):
            at = done[:, c * rows : (c + 1) * rows]
            hit = (c0 + c) - step_s[...] == j_lane
            for h in range(2):
                got = jnp.take_along_axis(at, pick_low + 8 * h, axis=1)
                where = slice(h * 128, (h + 1) * 128)
                pieces[:, where] = jnp.where(hit, got, pieces[:, where])

    for_left, own = unmixed(pieces[...])
    left_piece[...] = for_left
    back = pltpu.make_async_remote_copy(
        left_piece, ret_out, ret_send, ret_recv, device_id={"tile": left}, device_id_type=MESH
    )
    back.start()
    own_out[...] = own
    for copy in (side_fp, side_tr, side_meta):
        copy.wait_send()

    @pl.loop(0, n_chunk)
    def _(q):
        gone_out = buf.at[pl.ds(0, n_plane - 1), pl.ds(q * CHUNK, CHUNK)]
        pltpu.make_async_copy(gone_out, gone_out, send_sem.at[q]).wait()

    back.wait()


def body(slab_data, footprints, traces, corners, counts):
    n_tile, n_plane = lax.axis_size("tile"), lax.axis_size("plane")
    cols, frames, rows = slab_data.shape
    rows = rows // n_plane
    slots, box = footprints.shape
    span = traces.shape[1]
    both = 2 * slots
    any_space = pl.BlockSpec(memory_space=pltpu.HBM)
    vmem = pl.BlockSpec(memory_space=pltpu.VMEM)
    f32, bf16, i32 = jnp.float32, jnp.bfloat16, jnp.int32
    own, returned = pl.pallas_call(
        functools.partial(kernel, n_tile, n_plane),
        out_shape=(
            jax.ShapeDtypeStruct((slots, box), f32),
            jax.ShapeDtypeStruct((slots, box), f32),
        ),
        in_specs=[any_space] * 5,
        out_specs=(vmem, vmem),
        scratch_shapes=[
            pltpu.VMEM((n_plane, cols, frames, rows), bf16),
            pltpu.VMEM((slots, box), f32),
            pltpu.VMEM((slots, box), f32),
            pltpu.VMEM((slots, span), f32),
            pltpu.VMEM((slots, span), f32),
            pltpu.VMEM((2, slots), i32),
            pltpu.VMEM((8, 128), i32),
            pltpu.VMEM((8, 128), i32),
            pltpu.SMEM((1, 1), i32),
            pltpu.VMEM((both, box), f32),
            pltpu.VMEM((cols, both, rows), f32),
            pltpu.VMEM((both, rows), i32),
            pltpu.VMEM((both, rows), i32),
            pltpu.VMEM((GROUPS, both, 2 * both), bf16),
            pltpu.VMEM((both, box), f32),
            pltpu.VMEM((slots, box), f32),
            pltpu.SemaphoreType.DMA((4,)),
            pltpu.SemaphoreType.DMA((cols // CHUNK,)),
            pltpu.SemaphoreType.DMA((cols // CHUNK,)),
            pltpu.SemaphoreType.DMA((3,)),
            pltpu.SemaphoreType.DMA((3,)),
            pltpu.SemaphoreType.DMA,
            pltpu.SemaphoreType.DMA,
        ],
        compiler_params=pltpu.CompilerParams(
            collective_id=0, has_side_effects=True, vmem_limit_bytes=32 << 20
        ),
    )(slab_data, footprints, traces, corners.T, counts.reshape(1, 1))
    return own + returned


def solution(mesh):
    in_specs = (
        P("tile", "plane", None),
        P(("tile", "plane"), None),
        P(("tile", "plane"), None),
        P(("tile", "plane"), None),
        P(("tile", "plane")),
    )
    out_specs = P(("tile", "plane"), None)
    return jax.shard_map(body, mesh=mesh, in_specs=in_specs, out_specs=out_specs, check_vma=False)
```

time: 154 us -> 36.1 us (0.23)
  the two profiles are of different devices: /device:TPU:30 before, /device:TPU:31 now
where the time goes in v1:
time: 36.1 us; the launch traced here: 35.8 us
  Pallas kernels  31.2 us (86%)
  local copies, waits for them, and re-layouts  3.31 us (9%)
  between operations  0.67 us (2%)
  other arithmetic  0.64 us (2%)
    pallas_call x1, Pallas kernels, body(): pl.pallas_call(functools.partial(kernel, n_tile, n_plane), out_shape=(jax...  31.2 us
    unnamed x8, local copies, waits for them, and re-layouts  3.31 us

profile of v1, /device:TPU:31, one launch (start us, length us, event | category | flops | bytes accessed | tf_op | source)
XLA Modules:
  0.0 35.8 jit_solution(2919657958262879738)
XLA Ops:
  0.7 0.0 copy-start.3
  0.7 0.7 %copy-done.3 = s32[64,2]{0,1:T(2,128)S(1)} copy-done((s32[64,2]{0,1:T(2,128)S(1)}, s32[64,2]{0,1:T(2,128)}, u32[]{:S(2)}) %copy-start.3) | copy-done | bytes 536
  1.3 0.0 copy-start
  1.3 1.0 %copy-done = bf16[16,8,2048]{2,1,0:T(8,128)(2,1)S(1)} copy-done((bf16[16,8,2048]{2,1,0:T(8,128)(2,1)S(1)}, bf16[16,8,2048]{2,1,0:T(8,128)(2,1)}, u32[]{:S(2)}) %copy-start) | copy-done | bytes 524312
  2.4 0.0 copy-start.1
  2.4 0.8 %copy-done.1 = f32[64,256]{1,0:T(8,128)S(1)} copy-done((f32[64,256]{1,0:T(8,128)S(1)}, f32[64,256]{1,0:T(8,128)}, u32[]{:S(2)}) %copy-start.1) | copy-done | bytes 65560
  3.2 0.0 copy-start.2
  3.2 0.8 %copy-done.2 = f32[64,128]{1,0:T(8,128)S(1)} copy-done((f32[64,128]{1,0:T(8,128)S(1)}, f32[64,128]{1,0:T(8,128)}, u32[]{:S(2)}) %copy-start.2) | copy-done | bytes 32792
  4.0 31.2 %shard_map.55 = (f32[64,256]{1,0:T(8,128)S(1)}, f32[64,256]{1,0:T(8,128)S(1)}) custom-call(bf16[16,8,2048]{2,1,0:T(8,128)(2,1)S(1)} %copy-done, f32[64,256]{1,0:T(8,128)S(1)} %copy-done.1, f32[64,128]{1,0:T(8,128)S(1)} %copy-done.2, s32[2,64]{1,0:T(2,128)S(1)} %bitcast.3, s32[1,1]{1,0:T(1,128)} %bitcast.2.counts), custom_call_target="tpu_custom_call" | custom-call | tf_op jit(solution)/shard_map/pallas_call | solution.py:242
  35.2 0.6 %add.3 = f32[64,256]{1,0:T(8,128)} add(f32[64,256]{1,0:T(8,128)S(1)} %get-tuple-element.7, f32[64,256]{1,0:T(8,128)S(1)} %get-tuple-element.8) | non-fusion elementwise | flops 16384 | bytes 196608 | tf_op jit(solution)/shard_map/add | solution.py:279
Async XLA Ops:
  0.7 0.7 %copy-start.3 = (s32[64,2]{0,1:T(2,128)S(1)}, s32[64,2]{0,1:T(2,128)}, u32[]{:S(2)}) copy-start(s32[64,2]{0,1:T(2,128)} %param.8) | copy-start | bytes 1540
  1.3 1.0 %copy-start = (bf16[16,8,2048]{2,1,0:T(8,128)(2,1)S(1)}, bf16[16,8,2048]{2,1,0:T(8,128)(2,1)}, u32[]{:S(2)}) copy-start(bf16[16,8,2048]{2,1,0:T(8,128)(2,1)} %slab.1) | copy-start | bytes 1572868
  2.4 0.8 %copy-start.1 = (f32[64,256]{1,0:T(8,128)S(1)}, f32[64,256]{1,0:T(8,128)}, u32[]{:S(2)}) copy-start(f32[64,256]{1,0:T(8,128)} %fp.1) | copy-start | bytes 196612
  3.2 0.8 %copy-start.2 = (f32[64,128]{1,0:T(8,128)S(1)}, f32[64,128]{1,0:T(8,128)}, u32[]{:S(2)}) copy-start(f32[64,128]{1,0:T(8,128)} %tr.1) | copy-start | bytes 98308

commit v2 on v1

v2 whole, which is shorter than its diff:
```python
import functools

import jax
import jax.numpy as jnp
from jax import lax
from jax.experimental import pallas as pl
from jax.experimental.pallas import tpu as pltpu
from jax.sharding import PartitionSpec as P

PR = 16
PC = 16
SWEEPS = 2
GROUPS = 2
CHUNKS = ((0, 4), (4, 4), (8, 4), (12, 3), (15, 1))
LAST_LEFT = 3
X_SIZE = 4
LANES = 128
MESH = pl.DeviceIdType.MESH
GONE = 1 << 14


def mixed_order(left, own):
    half = own.shape[0] // GROUPS
    parts = []
    for g in range(GROUPS):
        parts += [left[g * half : (g + 1) * half], own[g * half : (g + 1) * half]]
    return jnp.concatenate(parts, axis=0)


def column_of(row):
    n = row.shape[1]
    eye = lax.broadcasted_iota(jnp.int32, (n, n), 0) == lax.broadcasted_iota(jnp.int32, (n, n), 1)
    spread = jnp.where(eye, jnp.broadcast_to(row.astype(jnp.float32), (n, n)), 0.0)
    return jnp.sum(spread, axis=1, keepdims=True).astype(jnp.int32)


def split(x):
    high = x.astype(jnp.bfloat16)
    return high, (x - high.astype(jnp.float32)).astype(jnp.bfloat16)


def kernel(
    n_tile, n_plane, slab, fp, tr, corners, counts, own_out, ret_out,
    buf, own_fp, nb_fp, own_tr, nb_tr, own_corner, own_meta, nb_meta, own_count,
    patch, first_mixed, later_high, later_low, row_at, first_at, pick_at, inverse_at,
    weights, trace_bf, left_piece,
    load_sem, send_sem, recv_sem, side_send, side_recv, ret_send, ret_recv, plane_in, side_in,
):
    cols, rows = buf.shape[1], buf.shape[3]
    slots = own_fp.shape[0]
    both = 2 * slots
    quarter = slots // GROUPS
    tile, me = lax.axis_index("tile"), lax.axis_index("plane")
    has_left, has_right = tile > 0, tile < n_tile - 1
    half = n_plane // 2
    place = jnp.where(me == 0, half - 1, jnp.where(me < half, me - 1, me))

    def plane_at(k):
        return jnp.where(k < half - 1, k + 1, jnp.where(k == half - 1, 0, k))

    left_first = has_left & (lax.rem(tile, X_SIZE) != 0)
    left_second = has_left & (lax.rem(tile, X_SIZE) == 0)
    right_second = has_right & (lax.rem(tile + 1, X_SIZE) != 0)
    right_first = has_right & (lax.rem(tile + 1, X_SIZE) == 0)

    barrier = pltpu.get_barrier_semaphore()

    @pl.loop(place + 1, n_plane)
    def _(k):
        pl.semaphore_signal(
            barrier, inc=1, device_id={"plane": plane_at(k)}, device_id_type=MESH
        )

    @pl.when(right_second)
    def _():
        pl.semaphore_signal(barrier, inc=1, device_id={"tile": tile + 1}, device_id_type=MESH)

    @pl.when(left_second)
    def _():
        pl.semaphore_signal(barrier, inc=1, device_id={"tile": tile - 1}, device_id_type=MESH)

    loads = [
        pltpu.make_async_copy(src, dst, load_sem.at[i])
        for i, (src, dst) in enumerate(
            ((corners, own_corner), (counts, own_count), (tr, own_tr), (fp, own_fp))
        )
    ]
    for load in loads:
        load.start()
    for q, (c0, n) in enumerate(CHUNKS):
        pltpu.make_async_copy(
            slab.at[pl.ds(c0, n), :, pl.ds(pl.multiple_of(me * rows, rows), rows)],
            buf.at[me, pl.ds(c0, n)],
            recv_sem.at[q],
        ).start()

    before = place + left_first.astype(jnp.int32) + right_first.astype(jnp.int32)

    @pl.when(before > 0)
    def _():
        pl.semaphore_wait(barrier, before)

    @pl.loop(0, place)
    def _(k):
        pl.semaphore_signal(
            plane_in.at[me], inc=1, device_id={"plane": plane_at(k)}, device_id_type=MESH
        )

    @pl.when(left_first)
    def _():
        pl.semaphore_signal(side_in.at[1], inc=1, device_id={"tile": tile - 1}, device_id_type=MESH)

    @pl.when(right_first)
    def _():
        pl.semaphore_signal(side_in.at[0], inc=1, device_id={"tile": tile + 1}, device_id_type=MESH)

    def send(q, peer):
        c0, n = CHUNKS[q]
        pltpu.make_async_remote_copy(
            slab.at[pl.ds(c0, n), :, pl.ds(pl.multiple_of(peer * rows, rows), rows)],
            buf.at[me, pl.ds(c0, n)],
            send_sem.at[q],
            recv_sem.at[q],
            device_id={"plane": peer},
            device_id_type=MESH,
        ).start()

    early = jnp.minimum(place, half)
    for a, b in ((0, early), (early, place)):
        for q in range(len(CHUNKS)):

            @pl.loop(a, b)
            def _(k, q=q):
                send(q, plane_at(k))

    def side(i, src, dst):
        return pltpu.make_async_remote_copy(
            src, dst, side_send.at[i], side_recv.at[i],
            device_id={"tile": tile + 1}, device_id_type=MESH,
        )

    side_fp, side_tr = side(0, fp, nb_fp), side(1, tr, nb_tr)
    side_meta = side(2, own_meta, nb_meta)
    loads[0].wait()
    loads[1].wait()
    lane = lax.broadcasted_iota(jnp.int32, (1, slots), 1)
    own_meta[...] = jnp.zeros_like(own_meta)
    own_meta[0:1, 0:slots] = own_corner[0:1, :]
    own_meta[1:2, 0:slots] = jnp.where(lane < own_count[0, 0], own_corner[1:2, :], GONE)

    @pl.when(right_second)
    def _():
        pl.semaphore_wait(side_in.at[1], 1)

    @pl.when(has_right)
    def _():
        side_meta.start()
        side_tr.start()
        side_fp.start()

    @pl.loop(place + 1, n_plane)
    def _(k):
        peer = plane_at(k)
        pl.semaphore_wait(plane_in.at[peer], 1)
        for q in range(len(CHUNKS)):
            send(q, peer)

    loads[2].wait()
    loads[3].wait()

    @pl.when(has_left)
    def _():
        side_meta.wait_recv()
        side_tr.wait_recv()
        side_fp.wait_recv()

    @pl.when(jnp.logical_not(has_left))
    def _():
        nb_meta[...] = jnp.full(nb_meta.shape, GONE, jnp.int32)
        nb_tr[...] = jnp.zeros_like(nb_tr)
        nb_fp[...] = jnp.zeros_like(nb_fp)

    top = mixed_order(column_of(nb_meta[0:1, 0:slots]), column_of(own_meta[0:1, 0:slots]))
    first = mixed_order(
        column_of(nb_meta[1:2, 0:slots]) - cols, column_of(own_meta[1:2, 0:slots])
    )
    alive = first < cols
    patch[...] = mixed_order(nb_fp[...], own_fp[...])
    trace = mixed_order(nb_tr[...], own_tr[...])
    gram = lax.dot_general(
        trace, trace, (((1,), (1,)), ((), ())),
        precision=lax.Precision.HIGHEST, preferred_element_type=jnp.float32,
    )
    eye = lax.broadcasted_iota(jnp.int32, (both, both), 0) == lax.broadcasted_iota(
        jnp.int32, (both, both), 1
    )
    diagonal = jnp.sum(jnp.where(eye, gram, 0.0), axis=1, keepdims=True)
    scale = jnp.where(alive, diagonal, 1.0)
    high, low = split(jnp.where(eye, 0.0, gram) / scale)
    for g in range(GROUPS):
        at = slice(g * slots, (g + 1) * slots)
        weights[g, 0:slots, 0:both] = high[at]
        weights[g, 0:slots, both : 2 * both] = high[at]
        weights[g, slots:both, 0:both] = low[at]
        weights[g, slots:both, both : 2 * both] = jnp.zeros((slots, both), jnp.bfloat16)
    trace_bf[...] = trace.astype(jnp.bfloat16)
    inverse_at[...] = jnp.broadcast_to(1.0 / scale, (both, rows))

    i_at = lax.broadcasted_iota(jnp.int32, (both, rows), 1) - top
    row_at[...] = jnp.where((i_at >= 0) & (i_at < PR), i_at, -1)
    first_at[...] = jnp.broadcast_to(first, (both, rows))
    lane_row = lax.broadcasted_iota(jnp.int32, (both, LANES), 1)
    pick_at[...] = jnp.broadcast_to(top, (both, LANES)) + (lane_row >> 4)

    def box_of(c):
        i_of = row_at[...]
        j_of = c - first_at[...]
        return i_of, j_of, (i_of >= 0) & (j_of >= 0) & (j_of < PC)

    def multiply(g, parts):
        stacked = jnp.concatenate([p[0] for p in parts] + [p[1] for p in parts], axis=0)
        product = jnp.dot(weights[g], stacked, preferred_element_type=jnp.float32)
        return product[0:slots] + product[slots:both]

    @pl.loop(0, cols // 2)
    def _(pair):
        highs, lows = [], []
        for c in (2 * pair, 2 * pair + 1):
            i_of, j_of, inside = box_of(c)
            at = (i_of & 7) * PC + (j_of & (PC - 1))
            lower = jnp.take_along_axis(patch[:, 0:LANES], at, axis=1)
            upper = jnp.take_along_axis(patch[:, LANES : 2 * LANES], at, axis=1)
            high, low = split(jnp.where(inside, jnp.where(i_of >= 8, upper, lower), 0.0))
            later_high[c] = high[slots:both]
            later_low[c] = low[slots:both]
            highs.append(high)
            lows.append(low)
        mixed = multiply(0, [(jnp.concatenate(highs, axis=1), jnp.concatenate(lows, axis=1))])
        first_mixed[2 * pair] = mixed[:, 0:rows]
        first_mixed[2 * pair + 1] = mixed[:, rows : 2 * rows]

    left_piece[...] = jnp.zeros_like(left_piece)
    own_out[...] = jnp.zeros_like(own_out)

    def take_back(c0, n, done, side_index, target):
        for g in range(GROUPS):
            a = g * slots + side_index * quarter
            j_lane = lax.broadcasted_iota(jnp.int32, (quarter, LANES), 1) & (PC - 1)
            for h in range(2):
                where = (slice(g * quarter, (g + 1) * quarter), slice(h * LANES, (h + 1) * LANES))
                sofar = target[where]
                for c in range(n):
                    got = jnp.take_along_axis(
                        done[a : a + quarter, c * rows : (c + 1) * rows],
                        pick_at[a : a + quarter, :] + 8 * h,
                        axis=1,
                    )
                    sofar = jnp.where(c0 + c - first_at[a : a + quarter, :] == j_lane, got, sofar)
                target[where] = sofar

    back = pltpu.make_async_remote_copy(
        left_piece, ret_out, ret_send, ret_recv, device_id={"tile": tile - 1}, device_id_type=MESH
    )
    for q, (c0, n) in enumerate(CHUNKS):
        landed = buf.at[:, pl.ds(c0, n)]
        pltpu.make_async_copy(landed, landed, recv_sem.at[q]).wait()
        data, signal = [], []
        for c in range(c0, c0 + n):
            block = buf[:, c].astype(jnp.float32)
            data.append(block.reshape(-1, rows).astype(jnp.bfloat16))
        summed = jnp.dot(
            trace_bf[...], jnp.concatenate(data, axis=1), preferred_element_type=jnp.float32
        )
        for c in range(n):
            _, _, inside = box_of(c0 + c)
            signal.append(
                jnp.where(inside, summed[:, c * rows : (c + 1) * rows] * inverse_at[...], -jnp.inf)
            )
        signal = jnp.concatenate(signal, axis=1)
        signal = [signal[g * slots : (g + 1) * slots] for g in range(GROUPS)]
        wide = lambda ref: jnp.concatenate([ref[c] for c in range(c0, c0 + n)], axis=1)
        now = [None] * GROUPS
        parts = [None] + [(wide(later_high), wide(later_low))]
        mixed = wide(first_mixed)
        for step in range(SWEEPS * GROUPS):
            g = step % GROUPS
            if step > 0:
                mixed = multiply(g, parts)
            now[g] = jnp.maximum(signal[g] - mixed, 0.0)
            parts[g] = split(now[g])
        done = jnp.concatenate(now, axis=0)
        if q <= LAST_LEFT:
            take_back(c0, n, done, 0, left_piece)
        if q == LAST_LEFT:

            @pl.when(left_second)
            def _():
                pl.semaphore_wait(side_in.at[0], 1)

            @pl.when(has_left)
            def _():
                back.start()

        take_back(c0, n, done, 1, own_out)

    @pl.when(has_right)
    def _():
        for copy in (side_fp, side_tr, side_meta):
            copy.wait_send()

    @pl.when(jnp.logical_not(has_right))
    def _():
        ret_out[...] = jnp.zeros_like(ret_out)

    for q, (c0, n) in enumerate(CHUNKS):
        gone_out = buf.at[pl.ds(0, n_plane - 1), pl.ds(c0, n)]
        pltpu.make_async_copy(gone_out, gone_out, send_sem.at[q]).wait()

    @pl.when(has_left)
    def _():
        back.wait_send()

    @pl.when(has_right)
    def _():
        back.wait_recv()


def body(slab_data, footprints, traces, corners, counts):
    n_tile, n_plane = lax.axis_size("tile"), lax.axis_size("plane")
    cols, frames, rows = slab_data.shape
    rows = rows // n_plane
    slots, box = footprints.shape
    span = traces.shape[1]
    both = 2 * slots
    hbm = pl.BlockSpec(memory_space=pltpu.HBM)
    vmem = pl.BlockSpec(memory_space=pltpu.VMEM)
    f32, bf16, i32 = jnp.float32, jnp.bfloat16, jnp.int32
    dma = pltpu.SemaphoreType.DMA
    regular = pltpu.SemaphoreType.REGULAR
    own, returned = pl.pallas_call(
        functools.partial(kernel, n_tile, n_plane),
        out_shape=(
            pltpu.VMEM((slots, box), f32),
            pltpu.VMEM((slots, box), f32),
        ),
        in_specs=[hbm] * 5,
        out_specs=(vmem, vmem),
        scratch_shapes=[
            pltpu.VMEM((n_plane, cols, frames, rows), bf16),
            pltpu.VMEM((slots, box), f32),
            pltpu.VMEM((slots, box), f32),
            pltpu.VMEM((slots, span), f32),
            pltpu.VMEM((slots, span), f32),
            pltpu.VMEM((2, slots), i32),
            pltpu.VMEM((8, 128), i32),
            pltpu.VMEM((8, 128), i32),
            pltpu.SMEM((1, 1), i32),
            pltpu.VMEM((both, box), f32),
            pltpu.VMEM((cols, slots, rows), f32),
            pltpu.VMEM((cols, slots, rows), bf16),
            pltpu.VMEM((cols, slots, rows), bf16),
            pltpu.VMEM((both, rows), i32),
            pltpu.VMEM((both, rows), i32),
            pltpu.VMEM((both, LANES), i32),
            pltpu.VMEM((both, rows), f32),
            pltpu.VMEM((GROUPS, both, 2 * both), bf16),
            pltpu.VMEM((both, span), bf16),
            pltpu.VMEM((slots, box), f32),
            dma((4,)),
            dma((len(CHUNKS),)),
            dma((len(CHUNKS),)),
            dma((3,)),
            dma((3,)),
            dma,
            dma,
            regular((n_plane,)),
            regular((2,)),
        ],
        compiler_params=pltpu.CompilerParams(
            collective_id=0, has_side_effects=True, vmem_limit_bytes=60 << 20
        ),
    )(slab_data, footprints, traces, corners.T, counts.reshape(1, 1))
    return own + returned


def solution(mesh):
    in_specs = (
        P("tile", "plane", None),
        P(("tile", "plane"), None),
        P(("tile", "plane"), None),
        P(("tile", "plane"), None),
        P(("tile", "plane")),
    )
    out_specs = P(("tile", "plane"), None)
    return jax.shard_map(body, mesh=mesh, in_specs=in_specs, out_specs=out_specs, check_vma=False)
```

time: 36.1 us -> 30.4 us (0.84)
  the two profiles are of different devices: /device:TPU:31 before, /device:TPU:28 now
where the time goes in v2:
time: 30.4 us; the launch traced here: 30.2 us
  Pallas kernels  28.9 us (95%)
  between operations  0.66 us (2%)
  other arithmetic  0.64 us (2%)
    pallas_call x1, Pallas kernels, body(): pl.pallas_call(functools.partial(kernel, n_tile, n_plane), out_shape=(plt...  28.9 us
    add x1, other arithmetic, body(): return own + returned  0.64 us

profile of v2, /device:TPU:28, one launch (start us, length us, event | category | flops | bytes accessed | tf_op | source)
XLA Modules:
  0.0 30.2 jit_solution(2325053989413642172)
XLA Ops:
  0.7 28.9 %shard_map.55 = (f32[64,256]{1,0:T(8,128)S(1)}, f32[64,256]{1,0:T(8,128)S(1)}) custom-call(bf16[16,8,2048]{2,1,0:T(8,128)(2,1)} %slab.1, f32[64,256]{1,0:T(8,128)} %fp.1, f32[64,128]{1,0:T(8,128)} %tr.1, s32[2,64]{1,0:T(2,128)} %bitcast.3, s32[1,1]{1,0:T(1,128)} %bitcast.2.counts), custom_call_target="tpu_custom_call" | custom-call | tf_op jit(solution)/shard_map/pallas_call | solution.py:340
  29.6 0.6 %add.3 = f32[64,256]{1,0:T(8,128)} add(f32[64,256]{1,0:T(8,128)S(1)} %get-tuple-element.7, f32[64,256]{1,0:T(8,128)S(1)} %get-tuple-element.8) | non-fusion elementwise | flops 16384 | bytes 196608 | tf_op jit(solution)/shard_map/add | solution.py:383

commit v3 on v2

--- a/solution.py
+++ b/solution.py
@@ -11,8 +11,8 @@
 PC = 16
 SWEEPS = 2
 GROUPS = 2
-CHUNKS = ((0, 4), (4, 4), (8, 4), (12, 3), (15, 1))
-LAST_LEFT = 3
+CHUNKS = ((0, 8), (8, 4), (12, 4))
+BLOCK = 4
 X_SIZE = 4
 LANES = 128
 MESH = pl.DeviceIdType.MESH
@@ -40,10 +40,10 @@
 
 
 def kernel(
-    n_tile, n_plane, slab, fp, tr, corners, counts, own_out, ret_out,
+    n_tile, n_plane, slab, fp, tr, corners, counts, out,
     buf, own_fp, nb_fp, own_tr, nb_tr, own_corner, own_meta, nb_meta, own_count,
     patch, first_mixed, later_high, later_low, row_at, first_at, pick_at, inverse_at,
-    weights, trace_bf, left_piece,
+    weights, trace_bf, own_piece, left_piece, ret_piece,
     load_sem, send_sem, recv_sem, side_send, side_recv, ret_send, ret_recv, plane_in, side_in,
 ):
     cols, rows = buf.shape[1], buf.shape[3]
@@ -87,13 +87,6 @@
     ]
     for load in loads:
         load.start()
-    for q, (c0, n) in enumerate(CHUNKS):
-        pltpu.make_async_copy(
-            slab.at[pl.ds(c0, n), :, pl.ds(pl.multiple_of(me * rows, rows), rows)],
-            buf.at[me, pl.ds(c0, n)],
-            recv_sem.at[q],
-        ).start()
-
     before = place + left_first.astype(jnp.int32) + right_first.astype(jnp.int32)
 
     @pl.when(before > 0)
@@ -125,13 +118,21 @@
             device_id_type=MESH,
         ).start()
 
+    late = place >= half
     early = jnp.minimum(place, half)
-    for a, b in ((0, early), (early, place)):
+    for a, b in ((0, 2), (2, half), (half, n_plane)):
         for q in range(len(CHUNKS)):
 
-            @pl.loop(a, b)
+            @pl.loop(jnp.minimum(a, place), jnp.minimum(b, place))
             def _(k, q=q):
-                send(q, plane_at(k))
+                send(q, jnp.where(late, k, plane_at(k)))
+
+    for q, (c0, n) in enumerate(CHUNKS):
+        pltpu.make_async_copy(
+            slab.at[pl.ds(c0, n), :, pl.ds(pl.multiple_of(me * rows, rows), rows)],
+            buf.at[me, pl.ds(c0, n)],
+            recv_sem.at[q],
+        ).start()
 
     def side(i, src, dst):
         return pltpu.make_async_remote_copy(
@@ -210,7 +211,7 @@
     row_at[...] = jnp.where((i_at >= 0) & (i_at < PR), i_at, -1)
     first_at[...] = jnp.broadcast_to(first, (both, rows))
     lane_row = lax.broadcasted_iota(jnp.int32, (both, LANES), 1)
-    pick_at[...] = jnp.broadcast_to(top, (both, LANES)) + (lane_row >> 4)
+    pick_at[...] = jnp.broadcast_to(top, (both, LANES)) + (lane_row & (PR - 1))
 
     def box_of(c):
         i_of = row_at[...]
@@ -239,31 +240,47 @@
         first_mixed[2 * pair] = mixed[:, 0:rows]
         first_mixed[2 * pair + 1] = mixed[:, rows : 2 * rows]
 
-    left_piece[...] = jnp.zeros_like(left_piece)
-    own_out[...] = jnp.zeros_like(own_out)
-
-    def take_back(c0, n, done, side_index, target):
+    lane = lax.broadcasted_iota(jnp.int32, (quarter, LANES), 1)
+    lane_spot = lane >> 4
+
+    def take_back(c0, n, done, which, target):
+        kept = target[c0 // BLOCK] if c0 % BLOCK else jnp.zeros((quarter, LANES), jnp.float32)
         for g in range(GROUPS):
-            a = g * slots + side_index * quarter
-            j_lane = lax.broadcasted_iota(jnp.int32, (quarter, LANES), 1) & (PC - 1)
+            a = g * slots + which * quarter
+            for c in range(n):
+                got = jnp.take_along_axis(
+                    done[a : a + quarter, c * rows : (c + 1) * rows],
+                    pick_at[a : a + quarter, :],
+                    axis=1,
+                )
+                kept = jnp.where(lane_spot == g * BLOCK + (c0 + c) % BLOCK, got, kept)
+        target[c0 // BLOCK] = kept
+
+    def back(b):
+        return pltpu.make_async_remote_copy(
+            left_piece.at[b], ret_piece.at[b], ret_send.at[b], ret_recv.at[b],
+            device_id={"tile": tile - 1}, device_id_type=MESH,
+        )
+
+    def place_back(b, pieces, sofar):
+        new = []
+        for g in range(GROUPS):
+            a = g * slots + quarter
             for h in range(2):
-                where = (slice(g * quarter, (g + 1) * quarter), slice(h * LANES, (h + 1) * LANES))
-                sofar = target[where]
-                for c in range(n):
-                    got = jnp.take_along_axis(
-                        done[a : a + quarter, c * rows : (c + 1) * rows],
-                        pick_at[a : a + quarter, :] + 8 * h,
-                        axis=1,
-                    )
-                    sofar = jnp.where(c0 + c - first_at[a : a + quarter, :] == j_lane, got, sofar)
-                target[where] = sofar
-
-    back = pltpu.make_async_remote_copy(
-        left_piece, ret_out, ret_send, ret_recv, device_id={"tile": tile - 1}, device_id_type=MESH
-    )
-    for q, (c0, n) in enumerate(CHUNKS):
-        landed = buf.at[:, pl.ds(c0, n)]
-        pltpu.make_async_copy(landed, landed, recv_sem.at[q]).wait()
+                column = first_at[a : a + quarter, :] + (lane & (PC - 1))
+                at = g * (BLOCK * PR) + (column & (BLOCK - 1)) * PR + (lane >> 4) + 8 * h
+                got = jnp.take_along_axis(pieces, at, axis=1)
+                new.append(jnp.where((column >> 2) == b, got, sofar[g * 2 + h]))
+        return new
+
+    n_block = cols // BLOCK
+    boxes = [jnp.zeros((quarter, LANES), jnp.float32)] * (2 * GROUPS)
+    for c0 in range(0, cols, BLOCK):
+        n = BLOCK
+        for q, (start, width) in enumerate(CHUNKS):
+            if start == c0:
+                landed = buf.at[:, pl.ds(start, width)]
+                pltpu.make_async_copy(landed, landed, recv_sem.at[q]).wait()
         data, signal = [], []
         for c in range(c0, c0 + n):
             block = buf[:, c].astype(jnp.float32)
@@ -289,19 +306,23 @@
             now[g] = jnp.maximum(signal[g] - mixed, 0.0)
             parts[g] = split(now[g])
         done = jnp.concatenate(now, axis=0)
-        if q <= LAST_LEFT:
+        if True:
             take_back(c0, n, done, 0, left_piece)
-        if q == LAST_LEFT:
+        if c0 == 0:
 
             @pl.when(left_second)
             def _():
                 pl.semaphore_wait(side_in.at[0], 1)
 
+        if (c0 + n) % BLOCK == 0:
+
             @pl.when(has_left)
-            def _():
-                back.start()
-
-        take_back(c0, n, done, 1, own_out)
+            def _(b=c0 // BLOCK):
+                back(b).start()
+
+        take_back(c0, n, done, 1, own_piece)
+        if (c0 + n) % BLOCK == 0:
+            boxes = place_back(c0 // BLOCK, own_piece[c0 // BLOCK], boxes)
 
     @pl.when(has_right)
     def _():
@@ -310,7 +331,18 @@
 
     @pl.when(jnp.logical_not(has_right))
     def _():
-        ret_out[...] = jnp.zeros_like(ret_out)
+        ret_piece[...] = jnp.zeros_like(ret_piece)
+
+    for b in range(n_block):
+
+        @pl.when(has_right)
+        def _(b=b):
+            back(b).wait_recv()
+
+        boxes = place_back(n_block + b, ret_piece[b], boxes)
+    for g in range(GROUPS):
+        for h in range(2):
+            out[g * quarter : (g + 1) * quarter, h * LANES : (h + 1) * LANES] = boxes[g * 2 + h]
 
     for q, (c0, n) in enumerate(CHUNKS):
         gone_out = buf.at[pl.ds(0, n_plane - 1), pl.ds(c0, n)]
@@ -318,11 +350,8 @@
 
     @pl.when(has_left)
     def _():
-        back.wait_send()
-
-    @pl.when(has_right)
-    def _():
-        back.wait_recv()
+        for b in range(n_block):
+            back(b).wait_send()
 
 
 def body(slab_data, footprints, traces, corners, counts):
@@ -337,14 +366,11 @@
     f32, bf16, i32 = jnp.float32, jnp.bfloat16, jnp.int32
     dma = pltpu.SemaphoreType.DMA
     regular = pltpu.SemaphoreType.REGULAR
-    own, returned = pl.pallas_call(
+    return pl.pallas_call(
         functools.partial(kernel, n_tile, n_plane),
-        out_shape=(
-            pltpu.VMEM((slots, box), f32),
-            pltpu.VMEM((slots, box), f32),
-        ),
+        out_shape=pltpu.VMEM((slots, box), f32),
         in_specs=[hbm] * 5,
-        out_specs=(vmem, vmem),
+        out_specs=vmem,
         scratch_shapes=[
             pltpu.VMEM((n_plane, cols, frames, rows), bf16),
             pltpu.VMEM((slots, box), f32),
@@ -365,14 +391,16 @@
             pltpu.VMEM((both, rows), f32),
             pltpu.VMEM((GROUPS, both, 2 * both), bf16),
             pltpu.VMEM((both, span), bf16),
-            pltpu.VMEM((slots, box), f32),
+            pltpu.VMEM((cols // BLOCK, slots // GROUPS, LANES), f32),
+            pltpu.VMEM((cols // BLOCK, slots // GROUPS, LANES), f32),
+            pltpu.VMEM((cols // BLOCK, slots // GROUPS, LANES), f32),
             dma((4,)),
             dma((len(CHUNKS),)),
             dma((len(CHUNKS),)),
             dma((3,)),
             dma((3,)),
-            dma,
-            dma,
+            dma((cols // BLOCK,)),
+            dma((cols // BLOCK,)),
             regular((n_plane,)),
             regular((2,)),
         ],
@@ -380,7 +408,6 @@
             collective_id=0, has_side_effects=True, vmem_limit_bytes=60 << 20
         ),
     )(slab_data, footprints, traces, corners.T, counts.reshape(1, 1))
-    return own + returned
 
 
 def solution(mesh):

time: 30.4 us -> 29.1 us (0.957)
  the two profiles are of different devices: /device:TPU:28 before, /device:TPU:157 now
where the time goes in v3:
time: 29.1 us; the launch traced here: 29 us
  Pallas kernels  27.7 us (95%)
  between operations  0.66 us (2%)
  local copies, waits for them, and re-layouts  0.63 us (2%)
    pallas_call x1, Pallas kernels, body(): pl.pallas_call(functools.partial(kernel, n_tile, n_plane), out_shape=pltp...  27.7 us
    unnamed x1, local copies, waits for them, and re-layouts  0.63 us

profile of v3, /device:TPU:157, one launch (start us, length us, event | category | flops | bytes accessed | tf_op | source)
XLA Modules:
  0.0 29.0 jit_solution(8757168973265065756)
XLA Ops:
  0.7 27.7 %shard_map.55 = f32[64,256]{1,0:T(8,128)S(1)} custom-call(bf16[16,8,2048]{2,1,0:T(8,128)(2,1)} %slab.1, f32[64,256]{1,0:T(8,128)} %fp.1, f32[64,128]{1,0:T(8,128)} %tr.1, s32[2,64]{1,0:T(2,128)} %bitcast.3, s32[1,1]{1,0:T(1,128)} %bitcast.2.counts), custom_call_target="tpu_custom_call" | custom-call | tf_op jit(solution)/shard_map/pallas_call | solution.py:369
  28.3 0.6 %copy.7 = f32[64,256]{1,0:T(8,128)} copy(f32[64,256]{1,0:T(8,128)S(1)} %shard_map.55) | data formatting | bytes 131072

commit v4 on v3

--- a/solution.py
+++ b/solution.py
@@ -44,7 +44,7 @@
     buf, own_fp, nb_fp, own_tr, nb_tr, own_corner, own_meta, nb_meta, own_count,
     patch, first_mixed, later_high, later_low, row_at, first_at, pick_at, inverse_at,
     weights, trace_bf, own_piece, left_piece, ret_piece,
-    load_sem, send_sem, recv_sem, side_send, side_recv, ret_send, ret_recv, plane_in, side_in,
+    load_sem, send_sem, recv_sem, side_send, side_recv, ret_send, ret_recv, plane_in, side_in, relay,
 ):
     cols, rows = buf.shape[1], buf.shape[3]
     slots = own_fp.shape[0]
@@ -55,6 +55,8 @@
     half = n_plane // 2
     place = jnp.where(me == 0, half - 1, jnp.where(me < half, me - 1, me))
 
+    late = place >= half
+
     def plane_at(k):
         return jnp.where(k < half - 1, k + 1, jnp.where(k == half - 1, 0, k))
 
@@ -75,7 +77,7 @@
     def _():
         pl.semaphore_signal(barrier, inc=1, device_id={"tile": tile + 1}, device_id_type=MESH)
 
-    @pl.when(left_second)
+    @pl.when(left_second & jnp.logical_not(late))
     def _():
         pl.semaphore_signal(barrier, inc=1, device_id={"tile": tile - 1}, device_id_type=MESH)
 
@@ -87,7 +89,8 @@
     ]
     for load in loads:
         load.start()
-    before = place + left_first.astype(jnp.int32) + right_first.astype(jnp.int32)
+    right_told = right_first & jnp.logical_not(late)
+    before = place + left_first.astype(jnp.int32) + right_told.astype(jnp.int32)
 
     @pl.when(before > 0)
     def _():
@@ -103,7 +106,7 @@
     def _():
         pl.semaphore_signal(side_in.at[1], inc=1, device_id={"tile": tile - 1}, device_id_type=MESH)
 
-    @pl.when(right_first)
+    @pl.when(right_told)
     def _():
         pl.semaphore_signal(side_in.at[0], inc=1, device_id={"tile": tile + 1}, device_id_type=MESH)
 
@@ -118,7 +121,6 @@
             device_id_type=MESH,
         ).start()
 
-    late = place >= half
     early = jnp.minimum(place, half)
     for a, b in ((0, 2), (2, half), (half, n_plane)):
         for q in range(len(CHUNKS)):
@@ -149,22 +151,70 @@
     own_meta[0:1, 0:slots] = own_corner[0:1, :]
     own_meta[1:2, 0:slots] = jnp.where(lane < own_count[0, 0], own_corner[1:2, :], GONE)
 
-    @pl.when(right_second)
+    @pl.when(right_second & jnp.logical_not(late))
     def _():
         pl.semaphore_wait(side_in.at[1], 1)
 
-    @pl.when(has_right)
+    @pl.when(has_right & jnp.logical_not(late))
     def _():
         side_meta.start()
         side_tr.start()
         side_fp.start()
 
-    @pl.loop(place + 1, n_plane)
-    def _(k):
-        peer = plane_at(k)
-        pl.semaphore_wait(plane_in.at[peer], 1)
-        for q in range(len(CHUNKS)):
-            send(q, peer)
+    def send_to_later(low, high):
+        @pl.loop(jnp.maximum(place + 1, low), jnp.maximum(place + 1, high))
+        def _(k):
+            peer = plane_at(k)
+            pl.semaphore_wait(plane_in.at[peer], 1)
+            for q in range(len(CHUNKS)):
+                send(q, peer)
+
+    quarter_planes = half // 2
+    low_helper, high_helper = me < 2, (me >= half - 2) & (me < half)
+    core = lax.rem(me, 2)
+
+    def pass_on(helper):
+        for i in range(quarter_planes // 2):
+
+            @pl.when(helper & left_second)
+            def _(i=i):
+                if i == 0:
+                    pl.semaphore_wait(side_in.at[0], 1)
+                pl.semaphore_signal(
+                    relay.at[i], inc=1, device_id={"tile": tile - 1}, device_id_type=MESH
+                )
+
+    def hand_on(helper, base):
+        for i in range(quarter_planes // 2):
+
+            @pl.when(helper & right_first)
+            def _(i=i):
+                pl.semaphore_wait(relay.at[i], 1)
+                pl.semaphore_signal(
+                    side_in.at[1], inc=1, device_id={"plane": base + 2 * i + core},
+                    device_id_type=MESH,
+                )
+
+    send_to_later(0, half + quarter_planes)
+    pass_on(high_helper)
+    send_to_later(half + quarter_planes, n_plane)
+    pass_on(low_helper)
+    hand_on(high_helper, half)
+    hand_on(low_helper, half + quarter_planes)
+
+    @pl.when((right_second | right_first) & late)
+    def _():
+        pl.semaphore_wait(side_in.at[1], 1)
+
+    @pl.when(right_first & late)
+    def _():
+        pl.semaphore_signal(side_in.at[0], inc=1, device_id={"tile": tile + 1}, device_id_type=MESH)
+
+    @pl.when(has_right & late)
+    def _():
+        side_meta.start()
+        side_tr.start()
+        side_fp.start()
 
     loads[2].wait()
     loads[3].wait()
@@ -310,7 +360,7 @@
             take_back(c0, n, done, 0, left_piece)
         if c0 == 0:
 
-            @pl.when(left_second)
+            @pl.when(left_second & jnp.logical_not(low_helper | high_helper))
             def _():
                 pl.semaphore_wait(side_in.at[0], 1)
 
@@ -403,6 +453,7 @@
             dma((cols // BLOCK,)),
             regular((n_plane,)),
             regular((2,)),
+            regular((n_plane // 8,)),
         ],
         compiler_params=pltpu.CompilerParams(
             collective_id=0, has_side_effects=True, vmem_limit_bytes=60 << 20

time: 29.1 us -> 28.7 us (0.986)
  the two profiles are of different devices: /device:TPU:157 before, /device:TPU:94 now
where the time goes in v4:
time: 28.7 us; the launch traced here: 28.5 us
  Pallas kernels  27.3 us (95%)
  between operations  0.66 us (2%)
  local copies, waits for them, and re-layouts  0.63 us (2%)
    pallas_call x1, Pallas kernels, body(): pl.pallas_call(functools.partial(kernel, n_tile, n_plane), out_shape=pltp...  27.3 us
    unnamed x1, local copies, waits for them, and re-layouts  0.63 us

profile of v4, /device:TPU:94, one launch (start us, length us, event | category | flops | bytes accessed | tf_op | source)
XLA Modules:
  0.0 28.5 jit_solution(15348492478496184562)
XLA Ops:
  0.7 27.3 %shard_map.55 = f32[64,256]{1,0:T(8,128)S(1)} custom-call(bf16[16,8,2048]{2,1,0:T(8,128)(2,1)} %slab.1, f32[64,256]{1,0:T(8,128)} %fp.1, f32[64,128]{1,0:T(8,128)} %tr.1, s32[2,64]{1,0:T(2,128)} %bitcast.3, s32[1,1]{1,0:T(1,128)} %bitcast.2.counts), custom_call_target="tpu_custom_call" | custom-call | tf_op jit(solution)/shard_map/pallas_call | solution.py:419
  27.9 0.6 %copy.7 = f32[64,256]{1,0:T(8,128)} copy(f32[64,256]{1,0:T(8,128)S(1)} %shard_map.55) | data formatting | bytes 131072

commit v5 on v4

--- a/solution.py
+++ b/solution.py
@@ -43,7 +43,7 @@
     n_tile, n_plane, slab, fp, tr, corners, counts, out,
     buf, own_fp, nb_fp, own_tr, nb_tr, own_corner, own_meta, nb_meta, own_count,
     patch, first_mixed, later_high, later_low, row_at, first_at, pick_at, inverse_at,
-    weights, trace_bf, own_piece, left_piece, ret_piece,
+    weights, trace_bf, left_piece, ret_piece,
     load_sem, send_sem, recv_sem, side_send, side_recv, ret_send, ret_recv, plane_in, side_in, relay,
 ):
     cols, rows = buf.shape[1], buf.shape[3]
@@ -293,18 +293,18 @@
     lane = lax.broadcasted_iota(jnp.int32, (quarter, LANES), 1)
     lane_spot = lane >> 4
 
-    def take_back(c0, n, done, which, target):
-        kept = target[c0 // BLOCK] if c0 % BLOCK else jnp.zeros((quarter, LANES), jnp.float32)
+    def take_back(done, which):
+        kept = jnp.zeros((quarter, LANES), jnp.float32)
         for g in range(GROUPS):
             a = g * slots + which * quarter
-            for c in range(n):
+            for c in range(BLOCK):
                 got = jnp.take_along_axis(
                     done[a : a + quarter, c * rows : (c + 1) * rows],
                     pick_at[a : a + quarter, :],
                     axis=1,
                 )
-                kept = jnp.where(lane_spot == g * BLOCK + (c0 + c) % BLOCK, got, kept)
-        target[c0 // BLOCK] = kept
+                kept = jnp.where(lane_spot == g * BLOCK + c, got, kept)
+        return kept
 
     def back(b):
         return pltpu.make_async_remote_copy(
@@ -312,42 +312,50 @@
             device_id={"tile": tile - 1}, device_id_type=MESH,
         )
 
-    def place_back(b, pieces, sofar):
-        new = []
+    def place_back(b, pieces):
         for g in range(GROUPS):
             a = g * slots + quarter
             for h in range(2):
                 column = first_at[a : a + quarter, :] + (lane & (PC - 1))
                 at = g * (BLOCK * PR) + (column & (BLOCK - 1)) * PR + (lane >> 4) + 8 * h
                 got = jnp.take_along_axis(pieces, at, axis=1)
-                new.append(jnp.where((column >> 2) == b, got, sofar[g * 2 + h]))
-        return new
+                where = (slice(g * quarter, (g + 1) * quarter), slice(h * LANES, (h + 1) * LANES))
+                out[where] = jnp.where((column >> 2) == b, got, out[where])
 
     n_block = cols // BLOCK
-    boxes = [jnp.zeros((quarter, LANES), jnp.float32)] * (2 * GROUPS)
-    for c0 in range(0, cols, BLOCK):
-        n = BLOCK
+    out[...] = jnp.zeros_like(out)
+
+    @pl.when(left_second & jnp.logical_not(low_helper | high_helper))
+    def _():
+        pl.semaphore_wait(side_in.at[0], 1)
+
+    @pl.loop(0, n_block)
+    def _(b):
         for q, (start, width) in enumerate(CHUNKS):
-            if start == c0:
+
+            @pl.when(b * BLOCK == start)
+            def _(q=q, start=start, width=width):
                 landed = buf.at[:, pl.ds(start, width)]
                 pltpu.make_async_copy(landed, landed, recv_sem.at[q]).wait()
+
+        columns = [b * BLOCK + c for c in range(BLOCK)]
         data, signal = [], []
-        for c in range(c0, c0 + n):
+        for c in columns:
             block = buf[:, c].astype(jnp.float32)
             data.append(block.reshape(-1, rows).astype(jnp.bfloat16))
         summed = jnp.dot(
             trace_bf[...], jnp.concatenate(data, axis=1), preferred_element_type=jnp.float32
         )
-        for c in range(n):
-            _, _, inside = box_of(c0 + c)
+        for i, c in enumerate(columns):
+            _, _, inside = box_of(c)
             signal.append(
-                jnp.where(inside, summed[:, c * rows : (c + 1) * rows] * inverse_at[...], -jnp.inf)
+                jnp.where(inside, summed[:, i * rows : (i + 1) * rows] * inverse_at[...], -jnp.inf)
             )
         signal = jnp.concatenate(signal, axis=1)
         signal = [signal[g * slots : (g + 1) * slots] for g in range(GROUPS)]
-        wide = lambda ref: jnp.concatenate([ref[c] for c in range(c0, c0 + n)], axis=1)
+        wide = lambda ref: jnp.concatenate([ref[c] for c in columns], axis=1)
         now = [None] * GROUPS
-        parts = [None] + [(wide(later_high), wide(later_low))]
+        parts = [None, (wide(later_high), wide(later_low))]
         mixed = wide(first_mixed)
         for step in range(SWEEPS * GROUPS):
             g = step % GROUPS
@@ -356,23 +364,13 @@
             now[g] = jnp.maximum(signal[g] - mixed, 0.0)
             parts[g] = split(now[g])
         done = jnp.concatenate(now, axis=0)
-        if True:
-            take_back(c0, n, done, 0, left_piece)
-        if c0 == 0:
-
-            @pl.when(left_second & jnp.logical_not(low_helper | high_helper))
-            def _():
-                pl.semaphore_wait(side_in.at[0], 1)
-
-        if (c0 + n) % BLOCK == 0:
-
-            @pl.when(has_left)
-            def _(b=c0 // BLOCK):
-                back(b).start()
-
-        take_back(c0, n, done, 1, own_piece)
-        if (c0 + n) % BLOCK == 0:
-            boxes = place_back(c0 // BLOCK, own_piece[c0 // BLOCK], boxes)
+        left_piece[b] = take_back(done, 0)
+
+        @pl.when(has_left)
+        def _():
+            back(b).start()
+
+        place_back(b, take_back(done, 1))
 
     @pl.when(has_right)
     def _():
@@ -383,16 +381,13 @@
     def _():
         ret_piece[...] = jnp.zeros_like(ret_piece)
 
-    for b in range(n_block):
-
+    @pl.loop(0, n_block)
+    def _(b):
         @pl.when(has_right)
-        def _(b=b):
+        def _():
             back(b).wait_recv()
 
-        boxes = place_back(n_block + b, ret_piece[b], boxes)
-    for g in range(GROUPS):
-        for h in range(2):
-            out[g * quarter : (g + 1) * quarter, h * LANES : (h + 1) * LANES] = boxes[g * 2 + h]
+        place_back(n_block + b, ret_piece[b])
 
     for q, (c0, n) in enumerate(CHUNKS):
         gone_out = buf.at[pl.ds(0, n_plane - 1), pl.ds(c0, n)]
@@ -443,7 +438,6 @@
             pltpu.VMEM((both, span), bf16),
             pltpu.VMEM((cols // BLOCK, slots // GROUPS, LANES), f32),
             pltpu.VMEM((cols // BLOCK, slots // GROUPS, LANES), f32),
-            pltpu.VMEM((cols // BLOCK, slots // GROUPS, LANES), f32),
             dma((4,)),
             dma((len(CHUNKS),)),
             dma((len(CHUNKS),)),

time: 28.7 us -> 28.7 us (level)
  no operation moved by 1% of the time
where the time goes in v5:
time: 28.7 us; the launch traced here: 28.6 us
  Pallas kernels  27.3 us (95%)
  between operations  0.66 us (2%)
  local copies, waits for them, and re-layouts  0.63 us (2%)
    pallas_call x1, Pallas kernels, body(): pl.pallas_call(functools.partial(kernel, n_tile, n_plane), out_shape=pltp...  27.3 us
    unnamed x1, local copies, waits for them, and re-layouts  0.63 us

profile of v5, /device:TPU:94, one launch (start us, length us, event | category | flops | bytes accessed | tf_op | source)
XLA Modules:
  0.0 28.6 jit_solution(7899881991447307024)
XLA Ops:
  0.7 27.3 %shard_map.55 = f32[64,256]{1,0:T(8,128)S(1)} custom-call(bf16[16,8,2048]{2,1,0:T(8,128)(2,1)} %slab.1, f32[64,256]{1,0:T(8,128)} %fp.1, f32[64,128]{1,0:T(8,128)} %tr.1, s32[2,64]{1,0:T(2,128)} %bitcast.3, s32[1,1]{1,0:T(1,128)} %bitcast.2.counts), custom_call_target="tpu_custom_call" | custom-call | tf_op jit(solution)/shard_map/pallas_call | solution.py:414
  27.9 0.6 %copy.7 = f32[64,256]{1,0:T(8,128)} copy(f32[64,256]{1,0:T(8,128)S(1)} %shard_map.55) | data formatting | bytes 131072

commit v6 on v5

--- a/solution.py
+++ b/solution.py
@@ -43,7 +43,7 @@
     n_tile, n_plane, slab, fp, tr, corners, counts, out,
     buf, own_fp, nb_fp, own_tr, nb_tr, own_corner, own_meta, nb_meta, own_count,
     patch, first_mixed, later_high, later_low, row_at, first_at, pick_at, inverse_at,
-    weights, trace_bf, left_piece, ret_piece,
+    weights, half_weights, trace_bf, left_piece, ret_piece,
     load_sem, send_sem, recv_sem, side_send, side_recv, ret_send, ret_recv, plane_in, side_in, relay,
 ):
     cols, rows = buf.shape[1], buf.shape[3]
@@ -254,6 +254,15 @@
         weights[g, 0:slots, both : 2 * both] = high[at]
         weights[g, slots:both, 0:both] = low[at]
         weights[g, slots:both, both : 2 * both] = jnp.zeros((slots, both), jnp.bfloat16)
+        for of in range(GROUPS):
+            src = slice(of * slots, (of + 1) * slots)
+            a = of * both
+            half_weights[g, 0:slots, a : a + slots] = high[at, src]
+            half_weights[g, 0:slots, a + slots : a + both] = high[at, src]
+            half_weights[g, slots:both, a : a + slots] = low[at, src]
+            half_weights[g, slots:both, a + slots : a + both] = jnp.zeros(
+                (slots, slots), jnp.bfloat16
+            )
     trace_bf[...] = trace.astype(jnp.bfloat16)
     inverse_at[...] = jnp.broadcast_to(1.0 / scale, (both, rows))
 
@@ -271,6 +280,14 @@
     def multiply(g, parts):
         stacked = jnp.concatenate([p[0] for p in parts] + [p[1] for p in parts], axis=0)
         product = jnp.dot(weights[g], stacked, preferred_element_type=jnp.float32)
+        return product[0:slots] + product[slots:both]
+
+    def multiply_part(g, of, part):
+        at = of * both
+        stacked = jnp.concatenate(part, axis=0)
+        product = jnp.dot(
+            half_weights[g, :, at : at + both], stacked, preferred_element_type=jnp.float32
+        )
         return product[0:slots] + product[slots:both]
 
     @pl.loop(0, cols // 2)
@@ -360,7 +377,9 @@
         for step in range(SWEEPS * GROUPS):
             g = step % GROUPS
             if step > 0:
-                mixed = multiply(g, parts)
+                mixed = older + multiply_part(g, 1 - g, parts[1 - g])
+            if step + 1 < SWEEPS * GROUPS:
+                older = multiply_part(1 - g, 1 - g, parts[1 - g])
             now[g] = jnp.maximum(signal[g] - mixed, 0.0)
             parts[g] = split(now[g])
         done = jnp.concatenate(now, axis=0)
@@ -435,6 +454,7 @@
             pltpu.VMEM((both, LANES), i32),
             pltpu.VMEM((both, rows), f32),
             pltpu.VMEM((GROUPS, both, 2 * both), bf16),
+            pltpu.VMEM((GROUPS, both, 2 * both), bf16),
             pltpu.VMEM((both, span), bf16),
             pltpu.VMEM((cols // BLOCK, slots // GROUPS, LANES), f32),
             pltpu.VMEM((cols // BLOCK, slots // GROUPS, LANES), f32),

time: 28.7 us -> 28.6 us (level)
  no operation moved by 1% of the time
where the time goes in v6:
time: 28.6 us; the launch traced here: 28.5 us
  Pallas kernels  27.2 us (95%)
  between operations  0.66 us (2%)
  local copies, waits for them, and re-layouts  0.63 us (2%)
    pallas_call x1, Pallas kernels, body(): pl.pallas_call(functools.partial(kernel, n_tile, n_plane), out_shape=pltp...  27.2 us
    unnamed x1, local copies, waits for them, and re-layouts  0.63 us

profile of v6, /device:TPU:94, one launch (start us, length us, event | category | flops | bytes accessed | tf_op | source)
XLA Modules:
  0.0 28.5 jit_solution(17642753827478930972)
XLA Ops:
  0.7 27.2 %shard_map.55 = f32[64,256]{1,0:T(8,128)S(1)} custom-call(bf16[16,8,2048]{2,1,0:T(8,128)(2,1)} %slab.1, f32[64,256]{1,0:T(8,128)} %fp.1, f32[64,128]{1,0:T(8,128)} %tr.1, s32[2,64]{1,0:T(2,128)} %bitcast.3, s32[1,1]{1,0:T(1,128)} %bitcast.2.counts), custom_call_target="tpu_custom_call" | custom-call | tf_op jit(solution)/shard_map/pallas_call | solution.py:433
  27.9 0.6 %copy.7 = f32[64,256]{1,0:T(8,128)} copy(f32[64,256]{1,0:T(8,128)S(1)} %shard_map.55) | data formatting | bytes 131072

commit v7 on v4

--- a/solution.py
+++ b/solution.py
@@ -43,7 +43,7 @@
     n_tile, n_plane, slab, fp, tr, corners, counts, out,
     buf, own_fp, nb_fp, own_tr, nb_tr, own_corner, own_meta, nb_meta, own_count,
     patch, first_mixed, later_high, later_low, row_at, first_at, pick_at, inverse_at,
-    weights, trace_bf, own_piece, left_piece, ret_piece,
+    weights, half_weights, trace_bf, own_piece, left_piece, ret_piece,
     load_sem, send_sem, recv_sem, side_send, side_recv, ret_send, ret_recv, plane_in, side_in, relay,
 ):
     cols, rows = buf.shape[1], buf.shape[3]
@@ -254,6 +254,15 @@
         weights[g, 0:slots, both : 2 * both] = high[at]
         weights[g, slots:both, 0:both] = low[at]
         weights[g, slots:both, both : 2 * both] = jnp.zeros((slots, both), jnp.bfloat16)
+        for of in range(GROUPS):
+            src = slice(of * slots, (of + 1) * slots)
+            a = of * both
+            half_weights[g, 0:slots, a : a + slots] = high[at, src]
+            half_weights[g, 0:slots, a + slots : a + both] = high[at, src]
+            half_weights[g, slots:both, a : a + slots] = low[at, src]
+            half_weights[g, slots:both, a + slots : a + both] = jnp.zeros(
+                (slots, slots), jnp.bfloat16
+            )
     trace_bf[...] = trace.astype(jnp.bfloat16)
     inverse_at[...] = jnp.broadcast_to(1.0 / scale, (both, rows))
 
@@ -271,6 +280,14 @@
     def multiply(g, parts):
         stacked = jnp.concatenate([p[0] for p in parts] + [p[1] for p in parts], axis=0)
         product = jnp.dot(weights[g], stacked, preferred_element_type=jnp.float32)
+        return product[0:slots] + product[slots:both]
+
+    def multiply_part(g, of, part):
+        at = of * both
+        stacked = jnp.concatenate(part, axis=0)
+        product = jnp.dot(
+            half_weights[g, :, at : at + both], stacked, preferred_element_type=jnp.float32
+        )
         return product[0:slots] + product[slots:both]
 
     @pl.loop(0, cols // 2)
@@ -352,7 +369,9 @@
         for step in range(SWEEPS * GROUPS):
             g = step % GROUPS
             if step > 0:
-                mixed = multiply(g, parts)
+                mixed = older + multiply_part(g, 1 - g, parts[1 - g])
+            if step + 1 < SWEEPS * GROUPS:
+                older = multiply_part(1 - g, 1 - g, parts[1 - g])
             now[g] = jnp.maximum(signal[g] - mixed, 0.0)
             parts[g] = split(now[g])
         done = jnp.concatenate(now, axis=0)
@@ -440,6 +459,7 @@
             pltpu.VMEM((both, LANES), i32),
             pltpu.VMEM((both, rows), f32),
             pltpu.VMEM((GROUPS, both, 2 * both), bf16),
+            pltpu.VMEM((GROUPS, both, 2 * both), bf16),
             pltpu.VMEM((both, span), bf16),
             pltpu.VMEM((cols // BLOCK, slots // GROUPS, LANES), f32),
             pltpu.VMEM((cols // BLOCK, slots // GROUPS, LANES), f32),

time: 28.7 us -> 28.6 us (level)
  no operation moved by 1% of the time
where the time goes in v7:
time: 28.6 us; the launch traced here: 28.5 us
  Pallas kernels  27.2 us (95%)
  between operations  0.66 us (2%)
  local copies, waits for them, and re-layouts  0.63 us (2%)
    pallas_call x1, Pallas kernels, body(): pl.pallas_call(functools.partial(kernel, n_tile, n_plane), out_shape=pltp...  27.2 us
    unnamed x1, local copies, waits for them, and re-layouts  0.63 us

profile of v7, /device:TPU:94, one launch (start us, length us, event | category | flops | bytes accessed | tf_op | source)
XLA Modules:
  0.0 28.5 jit_solution(6790947664280579289)
XLA Ops:
  0.7 27.2 %shard_map.55 = f32[64,256]{1,0:T(8,128)S(1)} custom-call(bf16[16,8,2048]{2,1,0:T(8,128)(2,1)} %slab.1, f32[64,256]{1,0:T(8,128)} %fp.1, f32[64,128]{1,0:T(8,128)} %tr.1, s32[2,64]{1,0:T(2,128)} %bitcast.3, s32[1,1]{1,0:T(1,128)} %bitcast.2.counts), custom_call_target="tpu_custom_call" | custom-call | tf_op jit(solution)/shard_map/pallas_call | solution.py:438
  27.8 0.6 %copy.7 = f32[64,256]{1,0:T(8,128)} copy(f32[64,256]{1,0:T(8,128)S(1)} %shard_map.55) | data formatting | bytes 131072
